TPU v7x, 32 devices: a whole 2x2x4 slice. The times are simulated.
32 devices in a mesh: dp: 4 (over x, core), seq: 8 (over z, y).
Axes of the slice: x: 2, y: 2, z: 4, core: 2. Of those that a mesh axis runs over, the one named last changes fastest.
Arguments:
- pipe_field: bfloat16 [4, 16384, 256], P('dp', 'seq'), may hold values from -6 to 6
- conv_weight: bfloat16 [3, 3, 256, 256], replicated, may hold values from -0.21875 to 0.21875
- conv_bias: float32 [3, 256], replicated, may hold values from -3 to 3
- norm_gain: float32 [256], replicated, may hold values from 0.1 to 1.9
- query_weight: bfloat16 [256, 256], replicated, may hold values from -0.18875 to 0.18875
- key_weight: bfloat16 [256, 256], replicated, may hold values from -5.6875 to 5.6875
- value_weight: bfloat16 [256, 256], replicated, may hold values from -0.375 to 0.375
- out_weight: bfloat16 [256, 256], replicated, may hold values from -0.375 to 0.375
- upstream: bfloat16 [4, 16384, 256], P('dp', 'seq'), may hold values from -0.0234375 to 0.0234375
Outputs:
- attended: float32 [4, 2048, 256], P('dp', 'seq')
- weight_grad: float32 [3, 3, 256, 256], replicated
- bias_grad: float32 [3, 256], replicated
All inputs are finite; a program needn't handle non-finite values.
Results may differ from a plain program's by a relative error of at most 0.03.
Values may be sent and summed in bfloat16 or wider, within the bound.
A program may use at most 128 MiB of HBM per device.

v0:
```python
import jax
import jax.numpy as jnp
from jax import lax
from jax.sharding import PartitionSpec as P

HEADS = 4
FIRST_SPACING = 2048
SECOND_SPACING = 4096
THIRD_SPACING = 8192
POOL = 8


def shifted(value, axis, steps):
    count = lax.axis_size(axis)
    initial, last = (max(0, -steps), min(count, count - steps))
    return lax.ppermute(value, axis, [(source, source + steps) for source in range(initial, last)])


def neighbours(block_rows, device_hops):
    lower_rows = shifted(block_rows, "seq", device_hops)
    upper_rows = shifted(block_rows, "seq", -device_hops)
    return (lower_rows, upper_rows)


def three_taps(lower_rows, middle_rows, upper_rows, weights_in):
    running = jnp.dot(lower_rows, weights_in[0], preferred_element_type=jnp.float32)
    running = running + jnp.dot(middle_rows, weights_in[1], preferred_element_type=jnp.float32)
    return running + jnp.dot(upper_rows, weights_in[2], preferred_element_type=jnp.float32)


def transposed(error_rows, weights_in):
    return lax.dot_general(
        error_rows, weights_in, (((1,), (1,)), ((), ())), preferred_element_type=jnp.float32
    )


def outer_sum(input_rows, error_rows):
    return lax.dot_general(
        input_rows, error_rows, (((0,), (0,)), ((), ())), preferred_element_type=jnp.float32
    )


def rms_scaled(values_in):
    return values_in * lax.rsqrt(jnp.mean(values_in * values_in, axis=-1, keepdims=True) + 1e-06)


def exact_product(left, right):
    return jnp.dot(
        left,
        right.astype(jnp.float32),
        precision=lax.Precision.HIGHEST,
        preferred_element_type=jnp.float32,
    )


def attend_block(state_tuple, query_heads, key_rows, value_rows, score_scale):
    row_peak, running, context_sum = state_tuple
    head_width = query_heads.shape[2]
    key_heads = key_rows.reshape(-1, HEADS, head_width)
    value_heads = value_rows.reshape(-1, HEADS, head_width)
    scores = (
        jnp.einsum(
            "qhd,khd->hqk",
            query_heads,
            key_heads,
            precision=lax.Precision.HIGHEST,
            preferred_element_type=jnp.float32,
        )
        * score_scale
    )
    new_peak = jnp.maximum(row_peak, jnp.max(scores, axis=-1))
    factor = jnp.exp(row_peak - new_peak)
    exponent = jnp.exp(scores - new_peak[..., None])
    running = running * factor + jnp.sum(exponent, axis=-1)
    block_sum = jnp.einsum(
        "hqk,khd->hqd",
        exponent.astype(jnp.bfloat16),
        value_heads,
        preferred_element_type=jnp.float32,
    )
    return (new_peak, running, context_sum * factor[..., None] + block_sum)


def attend(state_tuple, query_heads, key_rows, value_rows, score_scale):
    key_total = key_rows.shape[0]
    block_rows = 2048
    if block_rows == key_total:
        return attend_block(state_tuple, query_heads, key_rows, value_rows, score_scale)

    def block_step(position, current):
        row_start = position * block_rows
        key_part = lax.dynamic_slice_in_dim(key_rows, row_start, block_rows, 0)
        value_part = lax.dynamic_slice_in_dim(value_rows, row_start, block_rows, 0)
        return attend_block(current, query_heads, key_part, value_part, score_scale)

    return lax.fori_loop(0, key_total // block_rows, block_step, state_tuple)


def on_device(
    pipe_field,
    conv_weight,
    conv_bias,
    norm_gain,
    query_weight,
    key_weight,
    value_weight,
    out_weight,
    upstream,
):
    run_count, cell_count, channels = pipe_field.shape
    hidden = pipe_field.reshape(-1, channels)
    stored = []
    for layer_index, tap_spacing in enumerate((FIRST_SPACING, SECOND_SPACING, THIRD_SPACING)):
        device_hops = tap_spacing // cell_count
        lower_rows, upper_rows = neighbours(hidden, device_hops)
        preact = (
            three_taps(lower_rows, hidden, upper_rows, conv_weight[layer_index])
            + conv_bias[layer_index]
        )
        stored.append((hidden, lower_rows, upper_rows, preact, device_hops))
        hidden = (hidden.astype(jnp.float32) + jax.nn.silu(preact)).astype(jnp.bfloat16)
    pooled = jnp.mean(hidden.astype(jnp.float32).reshape(-1, POOL, channels), axis=1)
    normed = rms_scaled(pooled) * norm_gain
    pool_rows = normed.shape[0]
    head_width = channels // HEADS
    score_scale = head_width ** (-0.5)
    query_heads = exact_product(normed, query_weight).reshape(pool_rows, HEADS, head_width)
    initial = (
        jnp.full((HEADS, pool_rows), -1e30, jnp.float32),
        jnp.zeros((HEADS, pool_rows), jnp.float32),
        jnp.zeros((HEADS, pool_rows, head_width), jnp.float32),
    )
    key_local = exact_product(normed, key_weight)
    value_local = exact_product(normed, value_weight).astype(jnp.bfloat16)
    folded = attend(
        initial,
        query_heads,
        lax.all_gather(key_local.astype(jnp.bfloat16), "seq", axis=0, tiled=True).astype(
            jnp.float32
        ),
        lax.all_gather(value_local, "seq", axis=0, tiled=True),
        score_scale,
    )
    final_peak, running, context_sum = folded
    context = jnp.transpose(context_sum / running[..., None], (1, 0, 2)).reshape(
        pool_rows, channels
    )
    context_normed = rms_scaled(context).astype(jnp.bfloat16)
    attended = jnp.dot(context_normed, out_weight, preferred_element_type=jnp.float32)
    attended = attended.reshape(run_count, pool_rows, channels)
    cotangent = upstream.reshape(-1, channels)
    weight_parts = [None] * len(stored)
    bias_parts = [None] * len(stored)
    for layer_index in reversed(range(len(stored))):
        hidden_in, lower_rows, upper_rows, preact, device_hops = stored[layer_index]
        gate_sig = jax.nn.sigmoid(preact)
        errors = (
            cotangent.astype(jnp.float32) * gate_sig * (1.0 + preact * (1.0 - gate_sig))
        ).astype(jnp.bfloat16)
        weight_local = jnp.stack(
            [
                outer_sum(lower_rows, errors),
                outer_sum(hidden_in, errors),
                outer_sum(upper_rows, errors),
            ]
        )
        bias_local = jnp.sum(errors.astype(jnp.float32), axis=0)
        weight_parts[layer_index] = weight_local
        bias_parts[layer_index] = bias_local
        if layer_index > 0:
            error_lower, error_upper = neighbours(errors, device_hops)
            back_terms = transposed(error_upper, conv_weight[layer_index, 0])
            back_terms = back_terms + transposed(errors, conv_weight[layer_index, 1])
            back_terms = back_terms + transposed(error_lower, conv_weight[layer_index, 2])
            cotangent = (cotangent.astype(jnp.float32) + back_terms).astype(jnp.bfloat16)
    weight_grad = jnp.stack(weight_parts)
    bias_grad = jnp.stack(bias_parts)
    weight_grad, bias_grad = lax.psum((weight_grad, bias_grad), ("dp", "seq"))
    return (attended, weight_grad, bias_grad)


def solution(mesh):
    return jax.shard_map(
        on_device,
        mesh=mesh,
        in_specs=(P("dp", "seq", None), P(), P(), P(), P(), P(), P(), P(), P("dp", "seq", None)),
        out_specs=(P("dp", "seq", None), P(), P()),
        check_vma=False,
    )
```

profile of v0, /device:TPU:0, one launch (start us, length us, event | category | flops | bytes accessed | tf_op | source)
XLA Modules:
  0.0 419.3 jit_solution(2271214505865224678)
XLA Ops:
  9.5 5.6 %collective-permute-start = (bf16[2048,256]{1,0:T(8,128)(2,1)}, bf16[2048,256]{1,0:T(8,128)(2,1)S(1)}, u32[]{:S(2)}, u32[]{:S(2)}) collective-permute-start(bf16[2048,256]{1,0:T(8,128)(2,1)} %bitcast.160), channel_id=1, source_target_pairs={{0,1},{1,2},{2,3},{3,4},{4,5},{5,6},{6,7},{8,9},{9,10},{10,11},{11... | collective-permute-start | bytes 3145736 | tf_op jit(solution)/shard_map/ppermute | solution.py:16
  17.6 18.9 %collective-permute-done.1 = bf16[2048,256]{1,0:T(8,128)(2,1)S(1)} collective-permute-done((bf16[2048,256]{1,0:T(8,128)(2,1)}, bf16[2048,256]{1,0:T(8,128)(2,1)S(1)}, u32[]{:S(2)}, u32[]{:S(2)}) %collective-permute-start.1) | collective-permute-done | bytes 1048608 | tf_op jit(solution)/shard_map/ppermute | solution.py:16
  36.9 22.3 %collective-permute-done = bf16[2048,256]{1,0:T(8,128)(2,1)S(1)} collective-permute-done((bf16[2048,256]{1,0:T(8,128)(2,1)}, bf16[2048,256]{1,0:T(8,128)(2,1)S(1)}, u32[]{:S(2)}, u32[]{:S(2)}) %collective-permute-start) | collective-permute-done | bytes 1048608 | tf_op jit(solution)/shard_map/ppermute | solution.py:16
  62.7 4.6 %collective-permute-start.2 = (bf16[2048,256]{1,0:T(8,128)(2,1)S(1)}, bf16[2048,256]{1,0:T(8,128)(2,1)S(1)}, u32[]{:S(2)}, u32[]{:S(2)}) collective-permute-start(bf16[2048,256]{1,0:T(8,128)(2,1)S(1)} %get-tuple-element.21), channel_id=1, source_target_pairs={{0,2},{1,3},{2,4},{3,5},{4,6},{5,7},{8,10},{9,11},{10,12},{11,13},... | collective-permute-start | bytes 3145736 | tf_op jit(solution)/shard_map/ppermute | solution.py:16
  67.8 20.6 %collective-permute-done.3 = bf16[2048,256]{1,0:T(8,128)(2,1)S(1)} collective-permute-done((bf16[2048,256]{1,0:T(8,128)(2,1)S(1)}, bf16[2048,256]{1,0:T(8,128)(2,1)S(1)}, u32[]{:S(2)}, u32[]{:S(2)}) %collective-permute-start.3) | collective-permute-done | bytes 1048608 | tf_op jit(solution)/shard_map/ppermute | solution.py:16
  89.6 2.3 add_convert_fusion.1
  93.1 5.6 %collective-permute-start.4 = (bf16[2048,256]{1,0:T(8,128)(2,1)S(1)}, bf16[2048,256]{1,0:T(8,128)(2,1)S(1)}, u32[]{:S(2)}, u32[]{:S(2)}) collective-permute-start(bf16[2048,256]{1,0:T(8,128)(2,1)S(1)} %get-tuple-element.23), channel_id=1, source_target_pairs={{0,4},{1,5},{2,6},{3,7},{8,12},{9,13},{10,14},{11,15},{16,20},{17,... | collective-permute-start | bytes 3145736 | tf_op jit(solution)/shard_map/ppermute | solution.py:16
  99.2 42.0 %collective-permute-done.5 = bf16[2048,256]{1,0:T(8,128)(2,1)S(1)} collective-permute-done((bf16[2048,256]{1,0:T(8,128)(2,1)S(1)}, bf16[2048,256]{1,0:T(8,128)(2,1)S(1)}, u32[]{:S(2)}, u32[]{:S(2)}) %collective-permute-start.5) | collective-permute-done | bytes 1048608 | tf_op jit(solution)/shard_map/ppermute | solution.py:16
  142.2 3.6 convert_reduce_fusion
  147.0 2.8 convert_reduce_fusion.1
  149.8 2.5 collective-permute-start.7
  161.9 13.6 %collective-permute-done.7 = bf16[2048,256]{1,0:T(8,128)(2,1)} collective-permute-done((bf16[2048,256]{1,0:T(8,128)(2,1)S(1)}, bf16[2048,256]{1,0:T(8,128)(2,1)}, u32[]{:S(2)}, u32[]{:S(2)}) %collective-permute-start.7) | collective-permute-done | bytes 1048608 | tf_op jit(solution)/shard_map/ppermute | solution.py:16
  177.2 36.3 %collective-permute-done.6 = bf16[2048,256]{1,0:T(8,128)(2,1)} collective-permute-done((bf16[2048,256]{1,0:T(8,128)(2,1)S(1)}, bf16[2048,256]{1,0:T(8,128)(2,1)}, u32[]{:S(2)}, u32[]{:S(2)}) %collective-permute-start.6) | collective-permute-done | bytes 1048608 | tf_op jit(solution)/shard_map/ppermute | solution.py:16
  213.5 3.8 convert_reduce_fusion.2
  217.4 2.4 collective-permute-start.9
  227.5 3.1 fusion.49
  232.1 6.0 %multiply_reduce_fusion = (f32[4,256]{1,0:T(4,128)S(1)}, f32[4,256,2048]{2,1,0:T(8,128)}) fusion(f32[256,4,64]{0,2,1:T(8,128)S(1)} %bitcast.162, bf16[2048,4,64]{0,2,1:T(8,128)(2,1)S(1)} %bitcast.161), kind=kOutput, calls=%fused_computation.1 | convolution fusion | flops 1614806016 | bytes 9703424 | tf_op jit(solution)/shard_map/qhd,khd->hqk/dot_general | solution.py:62
  238.2 19.3 %all-gather.5.cloned.1.call-done = bf16[2048,256]{1,0:T(8,128)(2,1)} async-done(((bf16[256,256]{1,0:T(8,128)(2,1)}), bf16[2048,256]{1,0:T(8,128)(2,1)}) %all-gather.5.cloned.1.call-update) | async-done | bytes 1048592 | tf_op jit(solution)/shard_map/all_gather | solution.py:141
  259.0 4.4 %fusion = f32[4,256]{1,0:T(4,128)S(1)} fusion(f32[4,256,2048]{2,1,0:T(8,128)} %get-tuple-element.28, f32[4,256]{1,0:T(4,128)S(1)} %get-tuple-element.17), kind=kLoop, calls=%fused_computation.2 | loop fusion | flops 6290432 | bytes 8396800 | tf_op jit(solution)/shard_map/reduce_sum | solution.py:74
  265.6 2.5 convert_reduce_fusion.3
  272.3 5.1 %multiply_reduce_fusion.1 = (f32[256]{0:T(256)S(1)}, f32[256,4,64]{0,2,1:T(8,128)S(1)}) fusion(f32[256,4]{0,1:T(4,128)S(1)} %bitcast_add_fusion, bf16[2048,4,64]{0,2,1:T(8,128)(2,1)S(1)} %bitcast.163, f32[4,256,2048]{2,1,0:T(8,128)} %get-tuple-element.28, f32[4,256]{1,0:T(4,128)S(1)} %get-tuple-element.17, f32[256,4]{0,1:T(4,128)S(1)} %get-tuple-element.16), kind=kOutput, calls=%fused_computation.63 | convolution fusion | flops 274988800 | bytes 9712640 | tf_op jit(solution)/shard_map/hqk,khd->hqd/dot_general | solution.py:75
  278.3 41.9 %psum.15 = f32[3,256]{1,0:T(4,128)} all-reduce(f32[3,256]{1,0:T(4,128)S(1)} %pad_maximum_fusion.1), channel_id=1, replica_groups=mesh['dp'=4,'seq'=8] {'dp','seq'}, use_global_device_ids=true, to_apply=%region_9.10 | all-reduce | flops 768 | bytes 6144 | tf_op jit(solution)/shard_map/psum | solution.py:178
  320.2 88.6 %all-reduce.2.cloned.1.call-done = f32[3,3,256,256]{2,3,1,0:T(8,128)} async-done(((f32[3,3,256,256]{2,3,1,0:T(8,128)}), f32[3,3,256,256]{2,3,1,0:T(8,128)}) %all-reduce.2.cloned.1.call-update) | async-done | bytes 2359312 | tf_op jit(solution)/shard_map/psum | solution.py:178
  408.8 3.0 copy.38
  (113 shorter events, 42.5 us)
Async XLA Ops:
  8.0 138.0 %copy-start = (bf16[256,256]{1,0:T(8,128)(2,1)S(1)}, bf16[256,256]{1,0:T(8,128)(2,1)}, u32[]{:S(2)}) copy-start(bf16[256,256]{1,0:T(8,128)(2,1)} %param.14) | copy-start | bytes 393220
  8.0 28.4 %copy-start.6 = (bf16[3,3,256,256]{3,2,1,0:T(8,128)(2,1)S(1)}, bf16[3,3,256,256]{3,2,1,0:T(8,128)(2,1)}, u32[]{:S(2)}) copy-start(bf16[3,3,256,256]{3,2,1,0:T(8,128)(2,1)} %param.10) | copy-start | bytes 3538948
  8.0 222.6 %all-gather.3.cloned.1.call-start = ((), (), s32[]{:S(2)}) async-start(), calls=%async_computation | async-start | bytes 1179648 | tf_op jit(solution)/shard_map/all_gather | solution.py:138
  8.1 28.4 %collective-permute-start.1 = (bf16[2048,256]{1,0:T(8,128)(2,1)}, bf16[2048,256]{1,0:T(8,128)(2,1)S(1)}, u32[]{:S(2)}, u32[]{:S(2)}) collective-permute-start(bf16[2048,256]{1,0:T(8,128)(2,1)} %bitcast.159), channel_id=1, source_target_pairs={{1,0},{2,1},{3,2},{4,3},{5,4},{6,5},{7,6},{9,8},{10,9},{11,10},{12... | collective-permute-start | bytes 3145736 | tf_op jit(solution)/shard_map/ppermute | solution.py:16
  9.5 49.7 %collective-permute-start = (bf16[2048,256]{1,0:T(8,128)(2,1)}, bf16[2048,256]{1,0:T(8,128)(2,1)S(1)}, u32[]{:S(2)}, u32[]{:S(2)}) collective-permute-start(bf16[2048,256]{1,0:T(8,128)(2,1)} %bitcast.160), channel_id=1, source_target_pairs={{0,1},{1,2},{2,3},{3,4},{4,5},{5,6},{6,7},{8,9},{9,10},{10,11},{11... | collective-permute-start | bytes 3145736 | tf_op jit(solution)/shard_map/ppermute | solution.py:16
  17.5 41.6 %copy-start.2 = (bf16[1,2048,256]{2,1,0:T(8,128)(2,1)S(1)}, bf16[1,2048,256]{2,1,0:T(8,128)(2,1)}, u32[]{:S(2)}) copy-start(bf16[1,2048,256]{2,1,0:T(8,128)(2,1)} %param.9) | copy-start | bytes 3145732
  61.4 28.1 %copy-start.8 = (bf16[2048,256]{1,0:T(8,128)(2,1)}, bf16[2048,256]{1,0:T(8,128)(2,1)S(1)}, u32[]{:S(2)}) copy-start(bf16[2048,256]{1,0:T(8,128)(2,1)S(1)} %get-tuple-element.21) | copy-start | bytes 3145732
  61.4 27.0 %collective-permute-start.3 = (bf16[2048,256]{1,0:T(8,128)(2,1)S(1)}, bf16[2048,256]{1,0:T(8,128)(2,1)S(1)}, u32[]{:S(2)}, u32[]{:S(2)}) collective-permute-start(bf16[2048,256]{1,0:T(8,128)(2,1)S(1)} %get-tuple-element.21), channel_id=1, source_target_pairs={{2,0},{3,1},{4,2},{5,3},{6,4},{7,5},{10,8},{11,9},{12,10},{13,11},... | collective-permute-start | bytes 3145736 | tf_op jit(solution)/shard_map/ppermute | solution.py:16
  62.7 26.8 %collective-permute-start.2 = (bf16[2048,256]{1,0:T(8,128)(2,1)S(1)}, bf16[2048,256]{1,0:T(8,128)(2,1)S(1)}, u32[]{:S(2)}, u32[]{:S(2)}) collective-permute-start(bf16[2048,256]{1,0:T(8,128)(2,1)S(1)} %get-tuple-element.21), channel_id=1, source_target_pairs={{0,2},{1,3},{2,4},{3,5},{4,6},{5,7},{8,10},{9,11},{10,12},{11,13},... | collective-permute-start | bytes 3145736 | tf_op jit(solution)/shard_map/ppermute | solution.py:16
  91.8 50.3 %copy-start.13 = (bf16[2048,256]{1,0:T(8,128)(2,1)}, bf16[2048,256]{1,0:T(8,128)(2,1)S(1)}, u32[]{:S(2)}) copy-start(bf16[2048,256]{1,0:T(8,128)(2,1)S(1)} %get-tuple-element.23) | copy-start | bytes 3145732
  91.8 49.3 %collective-permute-start.5 = (bf16[2048,256]{1,0:T(8,128)(2,1)S(1)}, bf16[2048,256]{1,0:T(8,128)(2,1)S(1)}, u32[]{:S(2)}, u32[]{:S(2)}) collective-permute-start(bf16[2048,256]{1,0:T(8,128)(2,1)S(1)} %get-tuple-element.23), channel_id=1, source_target_pairs={{4,0},{5,1},{6,2},{7,3},{12,8},{13,9},{14,10},{15,11},{20,16},{21,... | collective-permute-start | bytes 3145736 | tf_op jit(solution)/shard_map/ppermute | solution.py:16
  93.1 48.4 %collective-permute-start.4 = (bf16[2048,256]{1,0:T(8,128)(2,1)S(1)}, bf16[2048,256]{1,0:T(8,128)(2,1)S(1)}, u32[]{:S(2)}, u32[]{:S(2)}) collective-permute-start(bf16[2048,256]{1,0:T(8,128)(2,1)S(1)} %get-tuple-element.23), channel_id=1, source_target_pairs={{0,4},{1,5},{2,6},{3,7},{8,12},{9,13},{10,14},{11,15},{16,20},{17,... | collective-permute-start | bytes 3145736 | tf_op jit(solution)/shard_map/ppermute | solution.py:16
  147.0 110.5 %all-gather.5.cloned.1.call-start = ((), (), s32[]{:S(2)}) async-start(), calls=%async_computation.1 | async-start | bytes 1179648 | tf_op jit(solution)/shard_map/all_gather | solution.py:141
  147.0 6.7 %copy-start.14 = (bf16[2048,256]{1,0:T(8,128)(2,1)S(1)}, bf16[2048,256]{1,0:T(8,128)(2,1)}, u32[]{:S(2)}) copy-start(bf16[2048,256]{1,0:T(8,128)(2,1)} %copy-done.13) | copy-start | bytes 3145732
  149.8 25.7 %collective-permute-start.7 = (bf16[2048,256]{1,0:T(8,128)(2,1)S(1)}, bf16[2048,256]{1,0:T(8,128)(2,1)}, u32[]{:S(2)}, u32[]{:S(2)}) collective-permute-start(bf16[2048,256]{1,0:T(8,128)(2,1)S(1)} %get-tuple-element.15), channel_id=1, source_target_pairs={{0,4},{1,5},{2,6},{3,7},{8,12},{9,13},{10,14},{11,15},{16,20},{17,... | collective-permute-start | bytes 3145736 | tf_op jit(solution)/shard_map/ppermute | solution.py:16
  152.4 61.1 %collective-permute-start.6 = (bf16[2048,256]{1,0:T(8,128)(2,1)S(1)}, bf16[2048,256]{1,0:T(8,128)(2,1)}, u32[]{:S(2)}, u32[]{:S(2)}) collective-permute-start(bf16[2048,256]{1,0:T(8,128)(2,1)S(1)} %get-tuple-element.15), channel_id=1, source_target_pairs={{4,0},{5,1},{6,2},{7,3},{12,8},{13,9},{14,10},{15,11},{20,16},{21,... | collective-permute-start | bytes 3145736 | tf_op jit(solution)/shard_map/ppermute | solution.py:16
  155.9 252.9 %all-reduce.2.cloned.1.call-start = ((), (), s32[]{:S(2)}) async-start(), calls=%async_computation.2 | async-start | bytes 4718592 | tf_op jit(solution)/shard_map/psum | solution.py:178
  161.8 51.7 %copy-start.7 = (bf16[1,2048,256]{2,1,0:T(8,128)(2,1)S(1)}, bf16[1,2048,256]{2,1,0:T(8,128)(2,1)}, u32[]{:S(2)}) copy-start(bf16[1,2048,256]{2,1,0:T(8,128)(2,1)} %param.17) | copy-start | bytes 3145732
  161.8 51.7 %copy-start.28 = (f32[2048,256]{1,0:T(8,128)S(1)}, f32[2048,256]{1,0:T(8,128)}, u32[]{:S(2)}) copy-start(f32[2048,256]{1,0:T(8,128)} %get-tuple-element.24) | copy-start | bytes 6291460
  213.5 7.7 %copy-start.9 = (bf16[2048,256]{1,0:T(8,128)(2,1)S(1)}, bf16[2048,256]{1,0:T(8,128)(2,1)}, u32[]{:S(2)}) copy-start(bf16[2048,256]{1,0:T(8,128)(2,1)} %copy-done.8) | copy-start | bytes 3145732
  217.4 7.4 %copy-start.24 = (bf16[2048,256]{1,0:T(8,128)(2,1)S(1)}, bf16[2048,256]{1,0:T(8,128)(2,1)}, u32[]{:S(2)}) copy-start(bf16[2048,256]{1,0:T(8,128)(2,1)} %copy-done.23) | copy-start | bytes 3145732
  217.4 46.1 %collective-permute-start.9 = (bf16[2048,256]{1,0:T(8,128)(2,1)}, bf16[2048,256]{1,0:T(8,128)(2,1)}, u32[]{:S(2)}, u32[]{:S(2)}) collective-permute-start(bf16[2048,256]{1,0:T(8,128)(2,1)} %get-tuple-element.13), channel_id=1, source_target_pairs={{0,2},{1,3},{2,4},{3,5},{4,6},{5,7},{8,10},{9,11},{10,12},{11,13},... | collective-permute-start | bytes 3145736 | tf_op jit(solution)/shard_map/ppermute | solution.py:16
  219.8 45.5 %collective-permute-start.8 = (bf16[2048,256]{1,0:T(8,128)(2,1)}, bf16[2048,256]{1,0:T(8,128)(2,1)}, u32[]{:S(2)}, u32[]{:S(2)}) collective-permute-start(bf16[2048,256]{1,0:T(8,128)(2,1)} %get-tuple-element.13), channel_id=1, source_target_pairs={{2,0},{3,1},{4,2},{5,3},{6,4},{7,5},{10,8},{11,9},{12,10},{13,11},... | collective-permute-start | bytes 3145736 | tf_op jit(solution)/shard_map/ppermute | solution.py:16
  278.3 133.6 %copy-start.1 = (bf16[256,256]{1,0:T(8,128)(2,1)S(1)}, bf16[256,256]{1,0:T(8,128)(2,1)}, u32[]{:S(2)}) copy-start(bf16[256,256]{1,0:T(8,128)(2,1)} %param.14) | copy-start | bytes 393220
  (19 other events, 55.3 us)
Sparse Core Ops, SparseCore 0:
  147.1 64.3 all-gather.2
  213.6 43.7 all-gather.4
Sparse Core Ops, SparseCore 1:
  272.3 136.5 all-reduce.1
where the time goes:
time: 420 us; the launch traced here: 419 us
  waiting for transfers between devices  262 us (62%)
  matrix products  51.6 us (12%)
  blocking collectives  41.9 us (10%)
  starting transfers between devices  27.6 us (7%)
  between operations  16 us (4%)
  other arithmetic  11 us (3%)
  local copies, waits for them, and re-layouts  8.91 us (2%)
    ppermute x10, waiting for transfers between devices, shifted(): lax.ppermute(value, axis, [(source, source + steps) for source in range(i...  154 us
    psum x1, waiting for transfers between devices, on_device(): weight_grad, bias_grad = lax.psum((weight_grad, bias_grad), ('dp', 'seq'))  88.6 us
    psum x1, blocking collectives, on_device(): weight_grad, bias_grad = lax.psum((weight_grad, bias_grad), ('dp', 'seq'))  41.9 us
    ppermute x10, starting transfers between devices, shifted(): lax.ppermute(value, axis, [(source, source + steps) for source in range(i...  27.4 us
    all_gather x1, waiting for transfers between devices, on_device(): lax.all_gather(value_local, 'seq', axis=0, tiled=True)  19.3 us
    dot_general x6, matrix products, transposed(): lax.dot_general(error_rows, weights_in, (((1,), (1,)), ((), ())), preferr...  14.3 us
    dot_general x9, matrix products, outer_sum(): lax.dot_general(input_rows, error_rows, (((0,), (0,)), ((), ())), preferr...  10.3 us
  transfers between devices with their start and end apart: 13, of which 9 were waited for; matrix products, arithmetic and copies ran while one was open for 12% of the time, Pallas kernels for 0%

commit v1 on v0

--- a/solution.py
+++ b/solution.py
@@ -96,6 +96,17 @@
     return lax.fori_loop(0, key_total // block_rows, block_step, state_tuple)
 
 
+def blocks_shifted(value, blocks):
+    pad = jnp.zeros((abs(blocks),) + value.shape[1:], value.dtype)
+    if blocks > 0:
+        return jnp.concatenate([pad, value[:-blocks]], axis=0)
+    return jnp.concatenate([value[-blocks:], pad], axis=0)
+
+
+def flat(value):
+    return value.reshape(-1, value.shape[-1])
+
+
 def on_device(
     pipe_field,
     conv_weight,
@@ -108,75 +119,83 @@
     upstream,
 ):
     run_count, cell_count, channels = pipe_field.shape
-    hidden = pipe_field.reshape(-1, channels)
+    devices = lax.axis_size("seq")
+    me = lax.axis_index("seq")
+    part = cell_count // devices
+
+    def swapped(value):
+        return lax.all_to_all(
+            value.reshape(devices, part, channels), "seq", 0, 0, tiled=True
+        )
+
+    hidden = swapped(pipe_field)
+    cotangent = swapped(upstream)
     stored = []
     for layer_index, tap_spacing in enumerate((FIRST_SPACING, SECOND_SPACING, THIRD_SPACING)):
-        device_hops = tap_spacing // cell_count
-        lower_rows, upper_rows = neighbours(hidden, device_hops)
+        hops = tap_spacing // cell_count
+        lower_rows = flat(blocks_shifted(hidden, hops))
+        upper_rows = flat(blocks_shifted(hidden, -hops))
         preact = (
-            three_taps(lower_rows, hidden, upper_rows, conv_weight[layer_index])
+            three_taps(lower_rows, flat(hidden), upper_rows, conv_weight[layer_index])
             + conv_bias[layer_index]
-        )
-        stored.append((hidden, lower_rows, upper_rows, preact, device_hops))
+        ).reshape(hidden.shape)
+        stored.append((hidden, lower_rows, upper_rows, preact, hops))
         hidden = (hidden.astype(jnp.float32) + jax.nn.silu(preact)).astype(jnp.bfloat16)
-    pooled = jnp.mean(hidden.astype(jnp.float32).reshape(-1, POOL, channels), axis=1)
+    pooled = jnp.mean(
+        hidden.astype(jnp.float32).reshape(devices, part // POOL, POOL, channels), axis=2
+    )
     normed = rms_scaled(pooled) * norm_gain
-    pool_rows = normed.shape[0]
     head_width = channels // HEADS
     score_scale = head_width ** (-0.5)
-    query_heads = exact_product(normed, query_weight).reshape(pool_rows, HEADS, head_width)
+    gathered = lax.all_gather(normed, "seq", axis=0)
+    mine = lax.dynamic_index_in_dim(gathered, me, 1, keepdims=False)
+    pool_rows = cell_count // POOL
+    query_heads = exact_product(flat(mine), query_weight).reshape(pool_rows, HEADS, head_width)
     initial = (
         jnp.full((HEADS, pool_rows), -1e30, jnp.float32),
         jnp.zeros((HEADS, pool_rows), jnp.float32),
         jnp.zeros((HEADS, pool_rows, head_width), jnp.float32),
     )
-    key_local = exact_product(normed, key_weight)
-    value_local = exact_product(normed, value_weight).astype(jnp.bfloat16)
-    folded = attend(
-        initial,
-        query_heads,
-        lax.all_gather(key_local.astype(jnp.bfloat16), "seq", axis=0, tiled=True).astype(
-            jnp.float32
-        ),
-        lax.all_gather(value_local, "seq", axis=0, tiled=True),
-        score_scale,
-    )
-    final_peak, running, context_sum = folded
+    keys = exact_product(flat(gathered), key_weight).astype(jnp.bfloat16).astype(jnp.float32)
+    values = exact_product(flat(gathered), value_weight).astype(jnp.bfloat16)
+    final_peak, running, context_sum = attend(initial, query_heads, keys, values, score_scale)
     context = jnp.transpose(context_sum / running[..., None], (1, 0, 2)).reshape(
         pool_rows, channels
     )
     context_normed = rms_scaled(context).astype(jnp.bfloat16)
     attended = jnp.dot(context_normed, out_weight, preferred_element_type=jnp.float32)
     attended = attended.reshape(run_count, pool_rows, channels)
-    cotangent = upstream.reshape(-1, channels)
     weight_parts = [None] * len(stored)
     bias_parts = [None] * len(stored)
     for layer_index in reversed(range(len(stored))):
-        hidden_in, lower_rows, upper_rows, preact, device_hops = stored[layer_index]
+        hidden_in, lower_rows, upper_rows, preact, hops = stored[layer_index]
         gate_sig = jax.nn.sigmoid(preact)
         errors = (
             cotangent.astype(jnp.float32) * gate_sig * (1.0 + preact * (1.0 - gate_sig))
         ).astype(jnp.bfloat16)
-        weight_local = jnp.stack(
+        rows = flat(errors)
+        weight_parts[layer_index] = jnp.concatenate(
             [
-                outer_sum(lower_rows, errors),
-                outer_sum(hidden_in, errors),
-                outer_sum(upper_rows, errors),
+                outer_sum(lower_rows, rows),
+                outer_sum(flat(hidden_in), rows),
+                outer_sum(upper_rows, rows),
             ]
         )
-        bias_local = jnp.sum(errors.astype(jnp.float32), axis=0)
-        weight_parts[layer_index] = weight_local
-        bias_parts[layer_index] = bias_local
+        bias_parts[layer_index] = jnp.sum(rows.astype(jnp.float32), axis=0, keepdims=True)
         if layer_index > 0:
-            error_lower, error_upper = neighbours(errors, device_hops)
-            back_terms = transposed(error_upper, conv_weight[layer_index, 0])
-            back_terms = back_terms + transposed(errors, conv_weight[layer_index, 1])
-            back_terms = back_terms + transposed(error_lower, conv_weight[layer_index, 2])
-            cotangent = (cotangent.astype(jnp.float32) + back_terms).astype(jnp.bfloat16)
-    weight_grad = jnp.stack(weight_parts)
-    bias_grad = jnp.stack(bias_parts)
-    weight_grad, bias_grad = lax.psum((weight_grad, bias_grad), ("dp", "seq"))
-    return (attended, weight_grad, bias_grad)
+            back_terms = transposed(flat(blocks_shifted(errors, -hops)), conv_weight[layer_index, 0])
+            back_terms = back_terms + transposed(rows, conv_weight[layer_index, 1])
+            back_terms = back_terms + transposed(
+                flat(blocks_shifted(errors, hops)), conv_weight[layer_index, 2]
+            )
+            cotangent = (
+                cotangent.astype(jnp.float32) + back_terms.reshape(cotangent.shape)
+            ).astype(jnp.bfloat16)
+    packed = jnp.concatenate(weight_parts + bias_parts)
+    packed = lax.psum(packed, ("dp", "seq"))
+    bias_rows = len(stored)
+    weight_grad = packed[:-bias_rows].reshape(conv_weight.shape)
+    return (attended, weight_grad, packed[-bias_rows:])
 
 
 def solution(mesh):

time: 420 us -> 322 us (0.77)
  waiting for transfers between devices: 262 us -> 170 us
  local copies, waits for them, and re-layouts: 8.91 us -> 58.9 us
  blocking collectives: 41.9 us -> 0 us
  starting transfers between devices: 27.6 us -> 11.7 us
  other arithmetic: 11 us -> 19.3 us
  matrix products: 51.6 us -> 44.9 us
    ppermute x10 -> x0, waiting for transfers between devices: 154 us -> none  [shifted(): lax.ppermute(value, axis, [(source, source + steps) for source in range(i...]
    psum x1, waiting for transfers between devices: 88.6 us -> 145 us  [on_device(): packed = lax.psum(packed, ('dp', 'seq'))]
    psum x1 -> x0, blocking collectives: 41.9 us -> none  [on_device(): weight_grad, bias_grad = lax.psum((weight_grad, bias_grad), ('dp', 'seq'))]
    ppermute x10 -> x0, starting transfers between devices: 27.4 us -> none  [shifted(): lax.ppermute(value, axis, [(source, source + steps) for source in range(i...]
    all_to_all x0 -> x2, waiting for transfers between devices: none -> 24.4 us  [swapped(): lax.all_to_all(value.reshape(devices, part, channels), 'seq', 0, 0, tiled...]
    all_gather x2 -> x1, waiting for transfers between devices: 19.3 us -> 0.01 us  [on_device(): gathered = lax.all_gather(normed, 'seq', axis=0)]
    reshape x0 -> x8, local copies, waits for them, and re-layouts: none -> 18.4 us  [the longest x3 7.66 us: on_device(): preact = (three_taps(lower_rows, flat(hidden), upper_rows, conv_weight[la...]
    concatenate x0 -> x11, local copies, waits for them, and re-layouts: none -> 12.8 us  [the longest x1 7.09 us: on_device(): packed = jnp.concatenate(weight_parts + bias_parts)]
  transfers between devices with their start and end apart: 13 -> 4, of which waited for: 9 -> 2; matrix products, arithmetic and copies ran while one was open for 12% -> 18% of each run, Pallas kernels for 0% -> 0%
where the time goes in v1:
time: 322 us; the launch traced here: 321 us
  waiting for transfers between devices  170 us (53%)
  local copies, waits for them, and re-layouts  58.9 us (18%)
  matrix products  44.9 us (14%)
  other arithmetic  19.3 us (6%)
  between operations  16 us (5%)
  starting transfers between devices  11.7 us (4%)
    psum x1, waiting for transfers between devices, on_device(): packed = lax.psum(packed, ('dp', 'seq'))  145 us
    all_to_all x2, waiting for transfers between devices, swapped(): lax.all_to_all(value.reshape(devices, part, channels), 'seq', 0, 0, tiled...  24.4 us
    unnamed x53, local copies, waits for them, and re-layouts  15.5 us
    all_to_all x2, starting transfers between devices, swapped(): lax.all_to_all(value.reshape(devices, part, channels), 'seq', 0, 0, tiled...  11.7 us
    reduce_sum x3, other arithmetic, on_device(): jnp.sum(rows.astype(jnp.float32), axis=0, keepdims=True)  11.5 us
    dot_general x6, matrix products, transposed(): lax.dot_general(error_rows, weights_in, (((1,), (1,)), ((), ())), preferr...  9.64 us
    reshape x3, local copies, waits for them, and re-layouts, on_device(): preact = (three_taps(lower_rows, flat(hidden), upper_rows, conv_weight[la...  7.66 us
    concatenate x1, local copies, waits for them, and re-layouts, on_device(): packed = jnp.concatenate(weight_parts + bias_parts)  7.09 us
  transfers between devices with their start and end apart: 4, of which 2 were waited for; matrix products, arithmetic and copies ran while one was open for 18% of the time, Pallas kernels for 0%

profile of v1, /device:TPU:0, one launch (start us, length us, event | category | flops | bytes accessed | tf_op | source)
XLA Modules:
  0.0 320.6 jit_solution(4536993215292234022)
XLA Ops:
  8.0 2.4 copy.71
  10.4 7.4 %all-to-all-start = ((bf16[8,256,256]{1,2,0:T(8,128)(2,1)}), bf16[8,256,256]{1,2,0:T(8,128)(2,1)S(1)}, u32[]{:S(2)}, u32[]{:S(2)}) async-start(bf16[8,256,256]{1,2,0:T(8,128)(2,1)} %copy.71), calls=%async_computation | async-start | bytes 2097152 | tf_op jit(solution)/shard_map/all_to_all | solution.py:127
  19.1 24.4 %all-to-all-done = bf16[8,256,256]{1,2,0:T(8,128)(2,1)S(1)} async-done(((bf16[8,256,256]{1,2,0:T(8,128)(2,1)}), bf16[8,256,256]{1,2,0:T(8,128)(2,1)S(1)}, u32[]{:S(2)}, u32[]{:S(2)}) %all-to-all-start) | async-done | bytes 1048608 | tf_op jit(solution)/shard_map/all_to_all | solution.py:127
  43.6 4.2 %all-to-all-start.1 = ((bf16[8,256,256]{1,2,0:T(8,128)(2,1)}), bf16[8,256,256]{1,2,0:T(8,128)(2,1)}, u32[]{:S(2)}, u32[]{:S(2)}) async-start(bf16[8,256,256]{1,2,0:T(8,128)(2,1)} %copy.89), calls=%async_computation.1 | async-start | bytes 2097152 | tf_op jit(solution)/shard_map/all_to_all | solution.py:127
  52.1 2.7 fusion.43
  55.3 2.1 convolution_add_fusion.9
  57.4 2.7 fusion.6
  60.1 2.9 copy.76
  63.0 2.3 add_convert_fusion.2
  77.0 2.3 add_convert_fusion.1
  83.0 2.1 concatenate.38.clone
  91.1 2.7 fusion.4
  93.7 3.0 copy.86
  96.7 4.5 %convert_reduce_fusion = (f32[256]{0:T(256)S(1)}, bf16[8,256,256]{1,2,0:T(8,128)(2,1)S(1)}, f32[8,256,256]{1,2,0:T(8,128)}) fusion(f32[8,256,256]{1,2,0:T(8,128)} %copy.86, bf16[8,256,256]{1,2,0:T(8,128)(2,1)} %all-to-all-done.1, bf16[8,256,256]{1,2,0:T(8,128)(2,1)S(1)} %add_convert_fusion.1), kind=kLoop, calls=%fused_computation.31 | loop fusion | flops 8912640 | bytes 7341056 | tf_op jit(solution)/shard_map/reduce_sum | solution.py:184
  114.5 3.4 %convert_reduce_fusion.1 = (f32[256]{0:T(256)S(1)}, bf16[8,256,256]{1,2,0:T(8,128)(2,1)S(1)}) fusion(f32[8,256,256]{1,2,0:T(8,128)} %copy.81, f32[8,256,256]{1,2,0:T(8,128)} %copy.94, bf16[8,256,256]{1,2,0:T(8,128)(2,1)} %all-to-all-done.1), kind=kLoop, calls=%fused_computation.32 | loop fusion | flops 7864064 | bytes 6292480 | tf_op jit(solution)/shard_map/reduce_sum | solution.py:184
  128.3 2.7 convolution_add_fusion
  131.0 3.1 copy.99
  134.0 3.6 %convert_reduce_fusion.2 = (f32[256]{0:T(256)S(1)}, bf16[8,256,256]{1,2,0:T(8,128)(2,1)S(1)}) fusion(f32[8,256,256]{1,2,0:T(8,128)S(1)} %copy-done.3, f32[8,256,256]{1,2,0:T(8,128)} %copy.99, f32[8,256,256]{1,2,0:T(8,128)} %copy.94, bf16[8,256,256]{1,2,0:T(8,128)(2,1)} %all-to-all-done.1), kind=kLoop, calls=%fused_computation.33 | loop fusion | flops 9436928 | bytes 8389632 | tf_op jit(solution)/shard_map/reduce_sum | solution.py:184
  139.4 7.1 %concatenate.43 = f32[2307,256]{1,0:T(8,128)} concatenate(f32[256,256]{1,0:T(8,128)S(1)} %convolution_bitcast_fusion.6, f32[256,256]{1,0:T(8,128)S(1)} %convolution_bitcast_fusion.9, f32[256,256]{1,0:T(8,128)S(1)} %convolution_bitcast_fusion.5, f32[256,256]{1,0:T(8,128)S(1)} %copy-done.14, f32[256,256]{1,0:T(8,128)S(1)} %convolution_bitcast_fusion.8, f32[256,256]{1,0:T(8,128)S(1)} %copy-done.15, ...), dimensions={0} | concatenate | bytes 4724736 | tf_op jit(solution)/shard_map/concatenate | solution.py:194
  146.5 2.1 copy.87
  150.3 145.2 %all-reduce.12.cloned.1.call-done = f32[2307,256]{1,0:T(8,128)} async-done(((f32[2307,256]{1,0:T(8,128)}), f32[2307,256]{1,0:T(8,128)}) %all-reduce.12.cloned.1.call-update) | async-done | bytes 2362384 | tf_op jit(solution)/shard_map/psum | solution.py:195
  296.8 3.2 %slice.133 = f32[2304,256]{1,0:T(8,128)} slice(f32[2307,256]{1,0:T(8,128)} %all-reduce.12.cloned.1.call-done), slice={[0:2304], [0:256]} | slice | bytes 4718592 | tf_op jit(solution)/shard_map/slice | solution.py:197
  300.1 3.0 convolution_convert_fusion
  304.7 3.9 %multiply_reduce_fusion = (f32[4,256]{1,0:T(4,128)S(1)}, f32[4,256,2048]{2,1,0:T(8,128)S(1)}) fusion(f32[256,4,64]{0,2,1:T(8,128)S(1)} %fusion.75, bf16[2048,4,64]{0,2,1:T(8,128)(2,1)S(1)} %bitcast.166), kind=kOutput, calls=%fused_computation.1 | convolution fusion | flops 1614806016 | bytes 9703424 | tf_op jit(solution)/shard_map/qhd,khd->hqk/dot_general | solution.py:62
  (116 shorter events, 61.7 us)
Async XLA Ops:
  8.0 292.1 %copy-start = (bf16[256,256]{1,0:T(8,128)(2,1)S(1)}, bf16[256,256]{1,0:T(8,128)(2,1)}, u32[]{:S(2)}) copy-start(bf16[256,256]{1,0:T(8,128)(2,1)} %param.15) | copy-start | bytes 393220
  8.0 9.8 %copy-start.13 = (bf16[1,2048,256]{2,1,0:T(8,128)(2,1)S(1)}, bf16[1,2048,256]{2,1,0:T(8,128)(2,1)}, u32[]{:S(2)}) copy-start(bf16[1,2048,256]{2,1,0:T(8,128)(2,1)} %param.17) | copy-start | bytes 3145732
  10.4 8.7 %copy-start.19 = (f32[3,256]{1,0:T(4,128)S(1)}, f32[3,256]{1,0:T(4,128)}, u32[]{:S(2)}) copy-start(f32[3,256]{1,0:T(4,128)} %param.11) | copy-start | bytes 9220
  10.4 33.2 %all-to-all-start = ((bf16[8,256,256]{1,2,0:T(8,128)(2,1)}), bf16[8,256,256]{1,2,0:T(8,128)(2,1)S(1)}, u32[]{:S(2)}, u32[]{:S(2)}) async-start(bf16[8,256,256]{1,2,0:T(8,128)(2,1)} %copy.71), calls=%async_computation | async-start | bytes 2097152 | tf_op jit(solution)/shard_map/all_to_all | solution.py:127
  43.6 19.4 %copy-start.1 = (bf16[8,256,256]{1,2,0:T(8,128)(2,1)}, bf16[8,256,256]{1,2,0:T(8,128)(2,1)S(1)}, u32[]{:S(2)}) copy-start(bf16[8,256,256]{1,2,0:T(8,128)(2,1)S(1)} %all-to-all-done) | copy-start | bytes 3145732
  43.6 53.1 %all-to-all-start.1 = ((bf16[8,256,256]{1,2,0:T(8,128)(2,1)}), bf16[8,256,256]{1,2,0:T(8,128)(2,1)}, u32[]{:S(2)}, u32[]{:S(2)}) async-start(bf16[8,256,256]{1,2,0:T(8,128)(2,1)} %copy.89), calls=%async_computation.1 | async-start | bytes 2097152 | tf_op jit(solution)/shard_map/all_to_all | solution.py:127
  47.8 247.7 %all-reduce.12.cloned.1.call-start = ((), (), s32[]{:S(2)}) async-start(), calls=%async_computation.3 | async-start | bytes 4734976 | tf_op jit(solution)/shard_map/psum | solution.py:195
  49.5 1.4 copy-start.8
  50.9 1.2 copy-start.9
  72.4 1.4 copy-start.6
  89.6 1.4 copy-start.5
  105.8 2.3 copy-start.10
  109.8 1.5 copy-start.7
  131.0 3.1 copy-start.3
  134.0 3.6 %copy-start.2 = (bf16[8,256,256]{1,2,0:T(8,128)(2,1)S(1)}, bf16[8,256,256]{1,2,0:T(8,128)(2,1)}, u32[]{:S(2)}) copy-start(bf16[8,256,256]{1,2,0:T(8,128)(2,1)} %copy-done.1) | copy-start | bytes 3145732
  138.2 1.0 copy-start.11
  138.2 1.0 copy-start.12
  138.2 1.1 copy-start.14
  138.2 1.2 copy-start.15
  146.5 153.6 %all-gather.2.cloned.1.call-start = ((), (), s32[]{:S(2)}) async-start(), calls=%async_computation.2 | async-start | bytes 2359296 | tf_op jit(solution)/shard_map/all_gather | solution.py:150
  148.7 1.5 copy-start.17
  300.1 3.0 copy-start.16
  300.1 3.0 copy-start.4
  310.3 2.0 copy-start.18
  (1 other events, 0.7 us)
Sparse Core Ops, SparseCore 0:
  146.6 148.9 all-reduce.11
Sparse Core Ops, SparseCore 1:
  150.3 53.9 all-gather.1

commit v2 on v1

--- a/solution.py
+++ b/solution.py
@@ -1,6 +1,10 @@
+import functools
+
 import jax
 import jax.numpy as jnp
 from jax import lax
+from jax.experimental import pallas as pl
+from jax.experimental.pallas import tpu as pltpu
 from jax.sharding import PartitionSpec as P
 
 HEADS = 4
@@ -198,9 +202,384 @@
     return (attended, weight_grad, packed[-bias_rows:])
 
 
+BF = jnp.bfloat16
+F32 = jnp.float32
+MESH = pl.DeviceIdType.MESH
+
+
+def flipped(bit, wanted):
+    return 1 - bit if wanted else bit
+
+
+def mm(left, right):
+    return jnp.dot(left, right, preferred_element_type=F32)
+
+
+def split_two(value):
+    high = value.astype(BF)
+    return high, (value - high.astype(F32)).astype(BF)
+
+
+def fused_kernel(
+    nb,
+    part,
+    hops,
+    x_hbm,
+    w_ref,
+    bias_ref,
+    gain_ref,
+    wq_ref,
+    wk_ref,
+    wv_ref,
+    wo_ref,
+    u_hbm,
+    att_ref,
+    wg_ref,
+    bg_ref,
+    *scratch,
+):
+    (hid, cot, err, pre, nrm, keys, vals, ctx, bsum, qh, ql) = scratch[:11]
+    (xs, xr, us, ur, loc, ns, nr) = scratch[11:18]
+    reduce_refs = [scratch[18 + 8 * c : 26 + 8 * c] for c in range(3)]
+    dp = lax.axis_index("dp")
+    me = lax.axis_index("seq")
+    xpos, core = dp // 2, dp % 2
+    zpos, ypos = me // 2, me % 2
+    z1, z0 = zpos // 2, zpos % 2
+    channels = x_hbm.shape[-1]
+    layers = len(hops)
+
+    def z_peer(k):
+        return flipped(z1, k >> 1) * 2 + flipped(z0, k & 1)
+
+    def plane_peer(k):
+        return flipped(xpos, k >> 1), flipped(ypos, k & 1)
+
+    def seq_peer(k):
+        return z_peer(k >> 1) * 2 + flipped(ypos, k & 1)
+
+    core_id = (xpos * 2 + (1 - core), me)
+    plane_ids = [None]
+    plane_q = [None]
+    for k in range(1, 4):
+        px, py = plane_peer(k)
+        plane_ids.append((px * 2 + core, zpos * 2 + py))
+        plane_q.append(px * 2 + py)
+    z_ids = [None] + [(dp, z_peer(k) * 2 + ypos) for k in range(1, 4)]
+    seq_ids = [None] + [(dp, seq_peer(k)) for k in range(1, nb)]
+    quad = xpos * 2 + ypos
+
+    barrier = pltpu.get_barrier_semaphore()
+    greeted = [core_id, plane_ids[2], plane_ids[3]] + seq_ids[1:]
+    for ident in greeted:
+        pl.semaphore_signal(barrier, inc=1, device_id=ident, device_id_type=MESH)
+    pl.semaphore_wait(barrier, len(greeted))
+
+    def remote(src, dst, ssem, rsem, ident):
+        return pltpu.make_async_remote_copy(
+            src_ref=src, dst_ref=dst, send_sem=ssem, recv_sem=rsem,
+            device_id=ident, device_id_type=MESH,
+        )
+
+    def exchange(src_hbm, dst, ssem, rsem):
+        copies = []
+        for k in range(1, nb):
+            peer = seq_peer(k)
+            copies.append(
+                remote(
+                    src_hbm.at[0, pl.ds(pl.multiple_of(peer * part, part), part)],
+                    dst.at[me], ssem.at[k], rsem.at[k], seq_ids[k],
+                )
+            )
+        return copies
+
+    x_copies = exchange(x_hbm, hid.at[0], xs, xr)
+    u_copies = exchange(u_hbm, cot, us, ur)
+    for copy in x_copies:
+        copy.start()
+    own_rows = pl.ds(pl.multiple_of(me * part, part), part)
+    x_own = pltpu.make_async_copy(x_hbm.at[0, own_rows], hid.at[0, me], loc.at[0])
+    u_own = pltpu.make_async_copy(u_hbm.at[0, own_rows], cot.at[me], loc.at[1])
+    x_own.start()
+    u_own.start()
+    for copy in x_copies:
+        copy.wait_send()
+    for copy in u_copies:
+        copy.start()
+    x_own.wait()
+    for copy in x_copies:
+        copy.wait_recv()
+
+    for layer in range(layers):
+        hop = hops[layer]
+        for s in range(nb):
+            total = mm(hid[layer, s], w_ref[layer, 1]) + bias_ref[layer : layer + 1]
+            if s - hop >= 0:
+                total = total + mm(hid[layer, s - hop], w_ref[layer, 0])
+            if s + hop < nb:
+                total = total + mm(hid[layer, s + hop], w_ref[layer, 2])
+            pre[layer, s] = total
+            active = total / (1.0 + jnp.exp(-total))
+            after = (hid[layer, s].astype(F32) + active).astype(BF)
+            if layer < layers - 1:
+                hid[layer + 1, s] = after
+            else:
+                pooled = jnp.mean(
+                    after.astype(F32).reshape(part // POOL, POOL, channels), axis=1
+                )
+                nrm[me, s] = rms_scaled(pooled) * gain_ref[...]
+
+    near = remote(nrm.at[me], nrm.at[me], ns.at[0], nr.at[0], z_ids[1])
+    far = remote(nrm.at[me], nrm.at[me], ns.at[1], nr.at[1], z_ids[2])
+    far.start()
+    near.start()
+    y_id = (dp, zpos * 2 + (1 - ypos))
+
+    def to_y(k):
+        place = nrm.at[z_peer(k) * 2 + ypos]
+        return remote(place, place, ns.at[3 + k], nr.at[3 + k], y_id)
+
+    sides = [to_y(k) for k in range(4)]
+    sides[0].start()
+    near_place = nrm.at[z_peer(2) * 2 + ypos]
+    relay = remote(near_place, near_place, ns.at[2], nr.at[2], z_ids[1])
+    far.wait_recv()
+    relay.start()
+    sides[2].start()
+    near.wait_recv()
+    sides[1].start()
+
+    copies_of = [None] * layers
+
+    def reduce_open(layer):
+        own, send, r1, s1, r2, r3, g, other = reduce_refs[layer][:8]
+        rows = own.shape[1]
+        main = rows if layer else rows - 16
+        ssem, rsem = sems_of[layer]
+        grad = wg_ref[layer].reshape(-1, channels)
+        left, right = grad[:, :128], grad[:, 128:]
+        mine = jnp.where(core == 0, left, right).reshape(16, main, 128)
+        theirs = jnp.where(core == 0, right, left).reshape(16, main, 128)
+        own[:, :main] = mine
+        send[:, :main] = theirs.astype(BF)
+        if main != rows:
+            own[:, main:] = jnp.zeros((16, 16, 128), F32)
+            send[:, main:] = jnp.zeros((16, 16, 128), BF)
+            low, high = bsum[:, :128], bsum[:, 128:]
+            own[0, main:] = jnp.where(core == 0, low, high)
+            send[0, main:] = jnp.where(core == 0, high, low).astype(BF)
+        first = [remote(send, r1, ssem.at[0], rsem.at[0], core_id)]
+        second = [
+            remote(
+                s1.at[pl.ds(plane_q[k] * 4, 4)], r2.at[k - 1],
+                ssem.at[k], rsem.at[k], plane_ids[k],
+            )
+            for k in range(1, 4)
+        ]
+        third = [
+            remote(
+                s1.at[quad * 4 + z_peer(k)], r3.at[k - 1],
+                ssem.at[3 + k], rsem.at[3 + k], z_ids[k],
+            )
+            for k in range(1, 4)
+        ]
+        mine_at = g.at[quad * 4 + zpos]
+        fourth = [
+            remote(mine_at, mine_at, ssem.at[6 + k], rsem.at[6 + k], z_ids[k])
+            for k in range(1, 4)
+        ]
+        group = g.at[pl.ds(quad * 4, 4)]
+        fifth = [
+            remote(group, group, ssem.at[9 + k], rsem.at[9 + k], plane_ids[k])
+            for k in range(1, 4)
+        ]
+        sixth = [remote(g, other, ssem.at[13], rsem.at[13], core_id)]
+        copies_of[layer] = [first, second, third, fourth, fifth, sixth]
+        for copy in first:
+            copy.start()
+
+    def reduce_step(layer, stage):
+        own, send, r1, s1, r2, r3, g, other = reduce_refs[layer][:8]
+        for copy in copies_of[layer][stage]:
+            copy.wait()
+        group = pl.ds(quad * 4, 4)
+        if stage == 0:
+            own[...] = own[...] + r1[...].astype(F32)
+            s1[...] = own[...].astype(BF)
+        elif stage == 1:
+            total = own[group] + r2[0].astype(F32) + r2[1].astype(F32) + r2[2].astype(F32)
+            own[group] = total
+            s1[group] = total.astype(BF)
+        elif stage == 2:
+            place = quad * 4 + zpos
+            total = own[place] + r3[0].astype(F32) + r3[1].astype(F32) + r3[2].astype(F32)
+            g[place] = total.astype(BF)
+        elif stage == 5:
+            rows = own.shape[1]
+            main = rows if layer else rows - 16
+            a, b = g[:, :main].astype(F32), other[:, :main].astype(F32)
+            low, high = jnp.where(core == 0, a, b), jnp.where(core == 0, b, a)
+            wg_ref[layer, :, :, :128] = low.reshape(3, channels, 128)
+            wg_ref[layer, :, :, 128:] = high.reshape(3, channels, 128)
+            if main != rows:
+                a, b = g[0, main:].astype(F32), other[0, main:].astype(F32)
+                bg_ref[:, :128] = jnp.where(core == 0, a, b)[:layers]
+                bg_ref[:, 128:] = jnp.where(core == 0, b, a)[:layers]
+        if stage < 5:
+            for copy in copies_of[layer][stage + 1]:
+                copy.start()
+
+    sem_refs = scratch[42:]
+    sems_of = [(sem_refs[2 * c], sem_refs[2 * c + 1]) for c in range(3)]
+
+    def backward(layer):
+        hop = hops[layer]
+        width = part
+        bias_total = jnp.zeros((1, channels), F32)
+        for s in range(nb):
+            v = pre[layer, s]
+            gate = 1.0 / (1.0 + jnp.exp(-v))
+            e = (cot[s].astype(F32) * gate * (1.0 + v * (1.0 - gate))).astype(BF)
+            err[s] = e
+            bias_total = bias_total + jnp.sum(e.astype(F32), axis=0, keepdims=True)
+        bsum[layer : layer + 1] = bias_total
+
+        def outer(first_block, err_block, count):
+            rows = hid[layer, first_block : first_block + count].reshape(count * width, channels)
+            errs = err[err_block : err_block + count].reshape(count * width, channels)
+            return outer_sum(rows, errs)
+
+        wg_ref[layer, 0] = outer(0, hop, nb - hop)
+        wg_ref[layer, 1] = outer(0, 0, nb)
+        wg_ref[layer, 2] = outer(hop, 0, nb - hop)
+        reduce_open(layer)
+        if layer == 0:
+            return
+        for s in range(nb):
+            total = cot[s].astype(F32) + transposed(err[s], w_ref[layer, 1])
+            if s + hop < nb:
+                total = total + transposed(err[s + hop], w_ref[layer, 0])
+            if s - hop >= 0:
+                total = total + transposed(err[s - hop], w_ref[layer, 2])
+            cot[s] = total.astype(BF)
+
+    bsum[...] = jnp.zeros(bsum.shape, F32)
+    u_own.wait()
+    for copy in u_copies:
+        copy.wait()
+    backward(2)
+    relay.wait_recv()
+    sides[3].start()
+    backward(1)
+    reduce_step(2, 0)
+    backward(0)
+    reduce_step(1, 0)
+    reduce_step(2, 1)
+
+    for copy in sides:
+        copy.wait_recv()
+    head_width = channels // HEADS
+    per = part // POOL
+    mine = nrm[:, pl.ds(me, 1)].reshape(nb * per, channels)
+    high, low = split_two(mine)
+    q = (mm(high, wq_ref[...]) + mm(low, wq_ref[...])) * head_width ** (-0.5)
+    q_high, q_low = split_two(q)
+    qh[...] = q_high
+    ql[...] = q_low
+    for d in range(nb):
+        high, low = split_two(nrm[d].reshape(nb * per, channels))
+        rows = slice(d * nb * per, (d + 1) * nb * per)
+        keys[rows] = (mm(high, wk_ref[...]) + mm(low, wk_ref[...])).astype(BF)
+        vals[rows] = (mm(high, wv_ref[...]) + mm(low, wv_ref[...])).astype(BF)
+    reduce_step(0, 0)
+    reduce_step(1, 1)
+    reduce_step(2, 2)
+
+    for head in range(HEADS):
+        lanes = slice(head * head_width, (head + 1) * head_width)
+        scores = transposed(qh[:, lanes], keys[:, lanes]) + transposed(ql[:, lanes], keys[:, lanes])
+        peak = jnp.max(scores, axis=-1, keepdims=True)
+        expo = jnp.exp(scores - peak)
+        den = jnp.sum(expo, axis=-1, keepdims=True)
+        ctx[:, lanes] = mm(expo.astype(BF), vals[:, lanes]) / den
+        reduce_step(0, 1 + head)
+        if head < 3:
+            reduce_step(1, 2 + head)
+        if head < 3:
+            reduce_step(2, 3 + head)
+        if head == 3:
+            reduce_step(1, 5)
+    att_ref[0] = mm(rms_scaled(ctx[...]).astype(BF), wo_ref[...])
+    reduce_step(0, 5)
+    for copy in [near, far, relay] + sides:
+        copy.wait_send()
+
+
+def fused(mesh, *args):
+    pipe_field, conv_weight = args[0], args[1]
+    cells, channels = pipe_field.shape[1:]
+    nb = mesh.shape["seq"]
+    part = cells // nb
+    layers = conv_weight.shape[0]
+    hops = tuple(h // cells for h in (FIRST_SPACING, SECOND_SPACING, THIRD_SPACING))
+    pool_rows = cells // POOL
+    per = part // POOL
+    dma = pltpu.SemaphoreType.DMA
+    vm = pltpu.VMEM
+    scratch = [
+        vm((layers, nb, part, channels), BF),
+        vm((nb, part, channels), BF),
+        vm((nb, part, channels), BF),
+        vm((layers, nb, part, channels), F32),
+        vm((nb, nb, per, channels), F32),
+        vm((nb * pool_rows, channels), BF),
+        vm((nb * pool_rows, channels), BF),
+        vm((pool_rows, channels), F32),
+        vm((16, channels), F32),
+        vm((pool_rows, channels), BF),
+        vm((pool_rows, channels), BF),
+        dma((nb,)), dma((nb,)), dma((nb,)), dma((nb,)), dma((2,)), dma((7,)), dma((7,)),
+    ]
+    for layer in range(layers):
+        rows = 3 * channels // 16 + (0 if layer else 16)
+        scratch += [
+            vm((16, rows, 128), F32),
+            vm((16, rows, 128), BF),
+            vm((16, rows, 128), BF),
+            vm((16, rows, 128), BF),
+            vm((3, 4, rows, 128), BF),
+            vm((3, rows, 128), BF),
+            vm((16, rows, 128), BF),
+            vm((16, rows, 128), BF),
+        ]
+    for layer in range(layers):
+        scratch += [dma((14,)), dma((14,))]
+    inner = pl.BlockSpec(memory_space=pltpu.VMEM)
+    outer = pl.BlockSpec(memory_space=pl.ANY)
+    gain = args[3].reshape(1, channels)
+    return pl.pallas_call(
+        functools.partial(fused_kernel, nb, part, hops),
+        out_shape=(
+            jax.ShapeDtypeStruct((1, pool_rows, channels), F32),
+            jax.ShapeDtypeStruct(conv_weight.shape, F32),
+            jax.ShapeDtypeStruct((layers, channels), F32),
+        ),
+        in_specs=[outer] + [inner] * 7 + [outer],
+        out_specs=(inner, inner, inner),
+        scratch_shapes=scratch,
+        compiler_params=pltpu.CompilerParams(
+            collective_id=0, has_side_effects=True, vmem_limit_bytes=50 * 1024 * 1024
+        ),
+        cost_estimate=pl.CostEstimate(
+            flops=9 * 10**9, bytes_accessed=8 * 10**6, transcendentals=6 * 10**6
+        ),
+    )(pipe_field, conv_weight, args[2], gain, *args[4:])
+
+
 def solution(mesh):
+    small = mesh.shape["seq"] == 8 and mesh.shape["dp"] == 4
     return jax.shard_map(
-        on_device,
+        functools.partial(fused, mesh) if small else on_device,
         mesh=mesh,
         in_specs=(P("dp", "seq", None), P(), P(), P(), P(), P(), P(), P(), P("dp", "seq", None)),
         out_specs=(P("dp", "seq", None), P(), P()),

time: 322 us -> 122 us (0.38)
  waiting for transfers between devices: 170 us -> 0 us
  Pallas kernels: 0 us -> 108 us
  local copies, waits for them, and re-layouts: 58.9 us -> 13.2 us
  matrix products: 44.9 us -> 0 us
  other arithmetic: 19.3 us -> 0 us
  between operations: 16 us -> 0.66 us
  starting transfers between devices: 11.7 us -> 0 us
    psum x1 -> x0, waiting for transfers between devices: 145 us -> none  [on_device(): packed = lax.psum(packed, ('dp', 'seq'))]
    pallas_call x0 -> x1, Pallas kernels: none -> 108 us  [fused(): pl.pallas_call(functools.partial(fused_kernel, nb, part, hops), out_shape...]
    dot_general x30 -> x0, matrix products: 44.9 us -> none  [the longest x6 9.64 us: transposed(): lax.dot_general(error_rows, weights_in, (((1,), (1,)), ((), ())), preferr...]
    all_to_all x2 -> x0, waiting for transfers between devices: 24.4 us -> none  [swapped(): lax.all_to_all(value.reshape(devices, part, channels), 'seq', 0, 0, tiled...]
    reshape x8 -> x0, local copies, waits for them, and re-layouts: 18.4 us -> none  [the longest x3 7.66 us: on_device(): preact = (three_taps(lower_rows, flat(hidden), upper_rows, conv_weight[la...]
    reduce_sum x6 -> x0, other arithmetic: 13.8 us -> none  [the longest x3 11.5 us: on_device(): jnp.sum(rows.astype(jnp.float32), axis=0, keepdims=True)]
    concatenate x11 -> x0, local copies, waits for them, and re-layouts: 12.8 us -> none  [the longest x1 7.09 us: on_device(): packed = jnp.concatenate(weight_parts + bias_parts)]
    all_to_all x2 -> x0, starting transfers between devices: 11.7 us -> none  [swapped(): lax.all_to_all(value.reshape(devices, part, channels), 'seq', 0, 0, tiled...]
  transfers between devices with their start and end apart: 4 -> 0, of which waited for: 2 -> 0; matrix products, arithmetic and copies ran while one was open for 18% -> 0% of each run, Pallas kernels for 0% -> 0%
where the time goes in v2:
time: 122 us
  Pallas kernels  108 us (89%)
  local copies, waits for them, and re-layouts  13.2 us (11%)
    pallas_call x1, Pallas kernels, fused(): pl.pallas_call(functools.partial(fused_kernel, nb, part, hops), out_shape...  108 us
    unnamed x21, local copies, waits for them, and re-layouts  13.2 us

profile of v2, /device:TPU:0, one launch (start us, length us, event | category | flops | bytes accessed | tf_op | source)
XLA Modules:
  0.0 121.7 jit_solution(16288353942851284885)
XLA Ops:
  0.6 0.0 copy-start
  0.6 1.3 %copy-done = bf16[3,3,256,256]{3,2,1,0:T(8,128)(2,1)S(1)} copy-done((bf16[3,3,256,256]{3,2,1,0:T(8,128)(2,1)S(1)}, bf16[3,3,256,256]{3,2,1,0:T(8,128)(2,1)}, u32[]{:S(2)}) %copy-start) | copy-done | bytes 1179672
  1.9 0.0 copy-start.1
  1.9 1.2 %copy-done.1 = bf16[1,2048,256]{2,1,0:T(8,128)(2,1)S(1)} copy-done((bf16[1,2048,256]{2,1,0:T(8,128)(2,1)S(1)}, bf16[1,2048,256]{2,1,0:T(8,128)(2,1)}, u32[]{:S(2)}) %copy-start.1) | copy-done | bytes 1048600
  3.1 0.0 copy-start.2
  3.1 1.2 %copy-done.2 = bf16[1,2048,256]{2,1,0:T(8,128)(2,1)S(1)} copy-done((bf16[1,2048,256]{2,1,0:T(8,128)(2,1)S(1)}, bf16[1,2048,256]{2,1,0:T(8,128)(2,1)}, u32[]{:S(2)}) %copy-start.2) | copy-done | bytes 1048600
  4.4 0.0 copy-start.3
  4.4 0.9 copy-done.3
  5.3 0.0 copy-start.4
  5.3 0.9 copy-done.4
  6.2 0.0 copy-start.5
  6.2 0.9 copy-done.5
  7.1 0.0 copy-start.6
  7.1 0.9 copy-done.6
  8.0 0.0 copy-start.7
  8.0 0.7 copy-done.7
  8.7 0.0 copy-start.8
  8.7 0.7 copy-done.8
  9.3 107.8 %shard_map.112 = (f32[1,256,256]{2,1,0:T(8,128)S(1)}, f32[3,3,256,256]{3,2,1,0:T(8,128)}, f32[3,256]{1,0:T(4,128)S(1)}) custom-call(bf16[1,2048,256]{2,1,0:T(8,128)(2,1)S(1)} %copy-done.1, bf16[3,3,256,256]{3,2,1,0:T(8,128)(2,1)S(1)} %copy-done, f32[3,256]{1,0:T(4,128)S(1)} %copy-done.7, f32[1,256]{1,0:T(1,128)S(1)} %bitcast.1, ...), custom_call_target="tpu_custom_call" | custom-call | flops 8999999488 | bytes 8000000 | tf_op jit(solution)/shard_map/pallas_call | solution.py:560
  117.2 0.7 copy.15
  117.9 3.2 %copy.16 = f32[3,3,256,256]{3,2,1,0:T(8,128)} copy(f32[3,3,256,256]{3,2,1,0:T(8,128)} %get-tuple-element.7) | data formatting | bytes 4718592
  121.1 0.6 copy.17
Async XLA Ops:
  0.6 1.3 %copy-start = (bf16[3,3,256,256]{3,2,1,0:T(8,128)(2,1)S(1)}, bf16[3,3,256,256]{3,2,1,0:T(8,128)(2,1)}, u32[]{:S(2)}) copy-start(bf16[3,3,256,256]{3,2,1,0:T(8,128)(2,1)} %w_ref.1) | copy-start | bytes 3538948
  1.9 1.2 %copy-start.1 = (bf16[1,2048,256]{2,1,0:T(8,128)(2,1)S(1)}, bf16[1,2048,256]{2,1,0:T(8,128)(2,1)}, u32[]{:S(2)}) copy-start(bf16[1,2048,256]{2,1,0:T(8,128)(2,1)} %x_hbm.1) | copy-start | bytes 3145732
  3.1 1.2 %copy-start.2 = (bf16[1,2048,256]{2,1,0:T(8,128)(2,1)S(1)}, bf16[1,2048,256]{2,1,0:T(8,128)(2,1)}, u32[]{:S(2)}) copy-start(bf16[1,2048,256]{2,1,0:T(8,128)(2,1)} %u_hbm.1) | copy-start | bytes 3145732
  4.4 0.9 copy-start.3
  5.3 0.9 copy-start.4
  6.2 0.9 copy-start.5
  7.1 0.9 copy-start.6
  8.0 0.7 copy-start.7
  8.7 0.7 copy-start.8

commit v3 on v2

--- a/solution.py
+++ b/solution.py
@@ -319,7 +319,7 @@
             if s + hop < nb:
                 total = total + mm(hid[layer, s + hop], w_ref[layer, 2])
             pre[layer, s] = total
-            active = total / (1.0 + jnp.exp(-total))
+            active = total * (0.5 + 0.5 * jnp.tanh(0.5 * total))
             after = (hid[layer, s].astype(F32) + active).astype(BF)
             if layer < layers - 1:
                 hid[layer + 1, s] = after
@@ -438,7 +438,7 @@
         bias_total = jnp.zeros((1, channels), F32)
         for s in range(nb):
             v = pre[layer, s]
-            gate = 1.0 / (1.0 + jnp.exp(-v))
+            gate = 0.5 + 0.5 * jnp.tanh(0.5 * v)
             e = (cot[s].astype(F32) * gate * (1.0 + v * (1.0 - gate))).astype(BF)
             err[s] = e
             bias_total = bias_total + jnp.sum(e.astype(F32), axis=0, keepdims=True)
@@ -568,7 +568,7 @@
         out_specs=(inner, inner, inner),
         scratch_shapes=scratch,
         compiler_params=pltpu.CompilerParams(
-            collective_id=0, has_side_effects=True, vmem_limit_bytes=50 * 1024 * 1024
+            collective_id=0, has_side_effects=True, vmem_limit_bytes=61 * 1024 * 1024
         ),
         cost_estimate=pl.CostEstimate(
             flops=9 * 10**9, bytes_accessed=8 * 10**6, transcendentals=6 * 10**6

time: 122 us -> 116 us (0.951)
  local copies, waits for them, and re-layouts: 13.2 us -> 5.49 us
  Pallas kernels: 108 us -> 110 us
    unnamed x21 -> x5, local copies, waits for them, and re-layouts: 13.2 us -> 5.49 us
    pallas_call x1, Pallas kernels: 108 us -> 110 us  [fused(): pl.pallas_call(functools.partial(fused_kernel, nb, part, hops), out_shape...]
where the time goes in v3:
time: 116 us
  Pallas kernels  110 us (95%)
  local copies, waits for them, and re-layouts  5.49 us (5%)
    pallas_call x1, Pallas kernels, fused(): pl.pallas_call(functools.partial(fused_kernel, nb, part, hops), out_shape...  110 us
    unnamed x5, local copies, waits for them, and re-layouts  5.49 us

profile of v3, /device:TPU:0, one launch (start us, length us, event | category | flops | bytes accessed | tf_op | source)
XLA Modules:
  0.0 115.7 jit_solution(2093244177032427788)
XLA Ops:
  0.6 109.6 %shard_map.112 = (f32[1,256,256]{2,1,0:T(8,128)}, f32[3,3,256,256]{3,2,1,0:T(8,128)}, f32[3,256]{1,0:T(4,128)}) custom-call(bf16[1,2048,256]{2,1,0:T(8,128)(2,1)} %x_hbm.1, bf16[3,3,256,256]{3,2,1,0:T(8,128)(2,1)} %w_ref.1, f32[3,256]{1,0:T(4,128)} %bias_ref.1, f32[1,256]{1,0:T(1,128)} %bitcast.1, bf16[256,256]{1,0:T(8,128)(2,1)} %wq_ref.1, ...), custom_call_target="tpu_custom_call" | custom-call | flops 8999999488 | bytes 8000000 | tf_op jit(solution)/shard_map/pallas_call | solution.py:560
  110.2 1.7 %copy.15 = f32[1,256,256]{2,1,0:T(8,128)} copy(f32[1,256,256]{2,1,0:T(8,128)} %get-tuple-element.6) | data formatting | bytes 524288
  111.9 0.0 copy-start
  111.9 3.2 %copy.16 = f32[3,3,256,256]{3,2,1,0:T(8,128)} copy(f32[3,3,256,256]{3,2,1,0:T(8,128)} %get-tuple-element.7) | data formatting | bytes 4718592
  115.1 0.0 copy-done
  115.1 0.6 copy.17
Async XLA Ops:
  111.9 3.2 %copy-start = (f32[3,256]{1,0:T(4,128)S(1)}, f32[3,256]{1,0:T(4,128)}, u32[]{:S(2)}) copy-start(f32[3,256]{1,0:T(4,128)} %get-tuple-element.8) | copy-start | bytes 9220
